TPU v7x, 512 devices: a whole 4x4x16 slice. The times are simulated.
512 devices in a mesh: grow: 16 (over z), gcol: 32 (over y, x, core).
Axes of the slice: x: 4, y: 4, z: 16, core: 2. Of those that a mesh axis runs over, the one named last changes fastest.
Arguments:
- pair_elements: float32 [2048, 16384], P(('grow', 'gcol')), may hold values from -0.5 to 0.5
- valence_index: int32 [2048], P(('grow', 'gcol')), may hold values from 0 to 4095
- conduction_index: int32 [2048], P(('grow', 'gcol')), may hold values from 0 to 32767
- valence_energy: float32 [4096], replicated, may hold values from -2 to -0.25
- conduction_energy: float32 [32768], replicated, may hold values from 0.25 to 2
- chi_in: float32 [16384, 16384], P('grow', 'gcol'), may hold values from -0.75 to 0.75
Outputs:
- chi_out: float32 [16384, 16384], P('grow', 'gcol')
All inputs are finite; a program needn't handle non-finite values.
Results may differ from a plain program's by a relative error of at most 0.00013.
Values sent between devices are 32-bit elements; how exact they have to be, the bound alone decides.
A program may use at most 64 MiB of HBM per device.

v0:
```python
import jax
import jax.numpy as jnp
from jax import lax
from jax.sharding import PartitionSpec as P


def lookup(indices, table):
    labels = jnp.arange(table.shape[0], dtype=jnp.int32)
    return jnp.sum(jnp.where(indices[:, None] == labels[None, :], table[None, :], 0.0), axis=1)


def outer_sum(left, right):
    return lax.dot_general(
        left,
        right,
        (((0,), (0,)), ((), ())),
        precision=lax.Precision.HIGHEST,
        preferred_element_type=jnp.float32,
    )


def per_device(
    pair_elements, valence_index, conduction_index, valence_energy, conduction_energy, chi_in
):
    column_count = lax.axis_size("gcol")
    weights = 4.0 / (
        lookup(conduction_index, conduction_energy) - lookup(valence_index, valence_energy)
    )
    local_pairs = pair_elements.shape[0]
    regrouped = lax.all_to_all(pair_elements, "gcol", split_axis=1, concat_axis=0, tiled=True)
    block_cols = regrouped.shape[1]
    layered = regrouped.reshape(column_count, 1, local_pairs, block_cols)
    column_panel = lax.all_gather(layered, "grow", axis=1, tiled=True).reshape(-1, block_cols)
    scaled = pair_elements * weights[:, None]
    row_rows = lax.all_to_all(scaled, "grow", split_axis=1, concat_axis=0, tiled=True)
    return chi_in + outer_sum(lax.all_gather(row_rows, "gcol", axis=0, tiled=True), column_panel)


def solution(mesh):
    placed = (
        P(("grow", "gcol"), None),
        P(("grow", "gcol")),
        P(("grow", "gcol")),
        P(),
        P(),
        P("grow", "gcol"),
    )
    return jax.shard_map(
        per_device, mesh=mesh, in_specs=placed, out_specs=P("grow", "gcol"), check_vma=False
    )
```

profile of v0, /device:TPU:1, one launch (start us, length us, event | category | flops | bytes accessed | tf_op | source)
XLA Modules:
  0.0 205.4 jit_solution(15527013311635948218)
XLA Ops:
  6.5 0.0 all-gather.6.cloned.1.call-start
  6.5 19.4 %all_to_all.35 = f32[4,32,512]{2,0,1:T(4,128)S(1)} all-to-all(f32[4,32,512]{2,0,1:T(4,128)} %bitcast.8), channel_id=1, replica_groups=mesh['grow'=16,'gcol'=32] {'gcol'}, dimensions={1} | all-to-all | bytes 524288 | tf_op jit(solution)/shard_map/all_to_all | solution.py:30
  25.9 0.8 copy.14
  26.7 0.0 all-gather.6.cloned.1.call-update
  26.8 0.0 all-gather.4.cloned.1.call-start
  26.8 0.9 select_reduce_fusion.1
  27.7 1.4 select_reduce_fusion
  29.1 1.1 broadcast_multiply_fusion
  30.2 31.4 %all_to_all.36 = f32[4,16,1024]{2,0,1:T(4,128)S(1)} all-to-all(f32[4,16,1024]{2,0,1:T(4,128)S(1)} %bitcast.9), channel_id=1, replica_groups=mesh['grow'=16,'gcol'=32] {'grow'}, dimensions={1} | all-to-all | bytes 524288 | tf_op jit(solution)/shard_map/all_to_all | solution.py:35
  61.6 0.8 all_to_all.29
  62.4 0.0 all-gather.4.cloned.1.call-update
  62.4 0.0 copy-start
  62.4 44.3 %all-gather.6.cloned.1.call-done = f32[32,64,512]{2,0,1:T(8,128)} async-done(((f32[32,4,512]{2,0,1:T(8,128)}), f32[32,64,512]{2,0,1:T(8,128)}) %all-gather.6.cloned.1.call-update) | async-done | bytes 4194320 | tf_op jit(solution)/shard_map/all_gather | solution.py:33
  106.8 6.6 %copy.15 = f32[32,64,512]{2,1,0:T(8,128)} copy(f32[32,64,512]{2,0,1:T(8,128)} %all-gather.6.cloned.1.call-done) | data formatting | bytes 8388608 | tf_op jit(solution)/shard_map/all_gather | solution.py:33
  113.3 67.2 %all-gather.4.cloned.1.call-done = f32[2048,1024]{1,0:T(8,128)} async-done(((f32[64,1024]{1,0:T(8,128)}), f32[2048,1024]{1,0:T(8,128)}) %all-gather.4.cloned.1.call-update) | async-done | bytes 8388624 | tf_op jit(solution)/shard_map/all_gather | solution.py:36
  180.5 0.0 copy-done
  180.5 18.0 %convolution_add_fusion = f32[1024,512]{1,0:T(8,128)} fusion(f32[1024,512]{1,0:T(8,128)S(1)} %copy-done, f32[2048,1024]{1,0:T(8,128)} %all-gather.4.cloned.1.call-done, f32[2048,512]{1,0:T(8,128)} %bitcast.7), kind=kOutput, calls=%fused_computation | convolution fusion | flops 12885426176 | bytes 16777216 | tf_op jit(solution)/shard_map/dot_general | solution.py:13
  (1 shorter events, 0.0 us)
Async XLA Ops:
  6.5 100.2 %all-gather.6.cloned.1.call-start = ((), (), s32[]{:S(2)}) async-start(), calls=%async_computation.3 | async-start | bytes 4456448 | tf_op jit(solution)/shard_map/all_gather | solution.py:33
  26.8 153.8 %all-gather.4.cloned.1.call-start = ((), (), s32[]{:S(2)}) async-start(), calls=%async_computation.2 | async-start | bytes 8650752 | tf_op jit(solution)/shard_map/all_gather | solution.py:36
  62.4 118.1 %copy-start = (f32[1024,512]{1,0:T(8,128)S(1)}, f32[1024,512]{1,0:T(8,128)}, u32[]{:S(2)}) copy-start(f32[1024,512]{1,0:T(8,128)} %param.11) | copy-start | bytes 6291460
Sparse Core Ops, SparseCore 0:
  26.9 79.8 all-gather.5
  109.9 70.5 all-gather.3
where the time goes:
time: 206 us; the launch traced here: 205 us
  waiting for transfers between devices  112 us (54%)
  blocking collectives  50.8 us (25%)
  matrix products  18 us (9%)
  between operations  13.4 us (7%)
  local copies, waits for them, and re-layouts  8.15 us (4%)
  other arithmetic  3.36 us (2%)
    all_gather x1, waiting for transfers between devices, per_device(): lax.all_gather(row_rows, 'gcol', axis=0, tiled=True)  67.2 us
    all_gather x1, waiting for transfers between devices, per_device(): lax.all_gather(layered, 'grow', axis=1, tiled=True).reshape(-1, block_cols)  44.3 us
    all_to_all x1, blocking collectives, per_device(): lax.all_to_all(scaled, 'grow', split_axis=1, concat_axis=0, tiled=True)  31.4 us
    all_to_all x1, blocking collectives, per_device(): lax.all_to_all(pair_elements, 'gcol', split_axis=1, concat_axis=0, tiled=...  19.4 us
    dot_general x1, matrix products, outer_sum(): lax.dot_general(left, right, (((0,), (0,)), ((), ())), precision=lax.Prec...  18 us
    all_gather x1, local copies, waits for them, and re-layouts, per_device(): lax.all_gather(layered, 'grow', axis=1, tiled=True).reshape(-1, block_cols)  6.56 us
  transfers between devices with their start and end apart: 2, of which 2 were waited for; matrix products, arithmetic and copies ran while one was open for 5% of the time, Pallas kernels for 0%

commit v1 on v0

v1 whole, which is shorter than its diff:
```python
import jax
import jax.numpy as jnp
from jax import lax
from jax.experimental import pallas as pl
from jax.experimental.pallas import tpu as pltpu
from jax.sharding import PartitionSpec as P

MESH = pl.DeviceIdType.MESH
PLANES = 16
PANELS = 32
PAIRS = 4
WIDTH = 512
SUBS = 4
DEEP = PANELS * PAIRS // SUBS
STEPS = 4 * (PLANES // 2) - 2
EDGES = (
    ((0, 0), (1, 0), (1, 2), (1, 3), (2, 0), (2, 1), (2, 2), (2, 3)),
    ((1, 0), (2, 0)),
    ((1, 1), (1, 2), (1, 3)),
    ((1, 0), (1, 3)),
)
MOVES = ((1, 0), (0, 1), (-1, 0), (0, -1))
DEEPEST = 5


def depths():
    found = {(0, 0): 0}
    for _ in range(16):
        for (da, db), nodes in zip(MOVES, EDGES):
            for a, b in nodes:
                if (a, b) in found:
                    found[((a + da) % 4, (b + db) % 4)] = found[(a, b)] + 1
    return found


DEPTHS = depths()
LAG = DEEPEST + 5


def wrap(value, size):
    return lax.rem(value + 4 * size, size)


def looked_up(table, index):
    place = lax.broadcasted_iota(jnp.int32, table.shape, 0) * 128 + lax.broadcasted_iota(
        jnp.int32, table.shape, 1
    )
    return jnp.sum(jnp.where(place == index, table, 0.0), axis=(0, 1), keepdims=True)


def split(value):
    high = value.astype(jnp.bfloat16)
    return high, (value - high.astype(jnp.float32)).astype(jnp.bfloat16)


def over_pairs(left, right):
    return lax.dot_general(
        left, right, (((0,), (0,)), ((), ())), preferred_element_type=jnp.float32
    )


def landed(ref, sem):
    pltpu.make_async_copy(ref, ref, sem).wait()


def kernel(
    valence_index, conduction_index, valence, conduction, elements, chi, out,
    outbox, inbox, cols, rows, cut,
    box_send, box_recv, ring_send, ring_recv, tree_send, tree_recv, twin_send, twin_recv, chi_sem,
):
    z = lax.axis_index("grow")
    c = lax.axis_index("gcol")
    core, x, y = lax.rem(c, 2), lax.rem(c // 2, 4), c // 8
    twin = c + 1 - 2 * core
    ahead, behind = wrap(z + 1, PLANES), wrap(z - 1, PLANES)

    barrier = pltpu.get_barrier_semaphore()

    @pl.loop(1, PANELS)
    def _(k):
        pl.semaphore_signal(
            barrier, inc=1, device_id={"gcol": wrap(c + k, PANELS)}, device_id_type=MESH
        )

    for side in (ahead, behind):
        pl.semaphore_signal(barrier, inc=1, device_id={"grow": side}, device_id_type=MESH)

    chi_copy = pltpu.make_async_copy(chi, out, chi_sem)
    chi_copy.start()

    pair = lax.broadcasted_iota(jnp.int32, (PAIRS, 1), 0)
    gaps = jnp.ones((PAIRS, 1), jnp.float32)
    for i in range(PAIRS):
        gap = looked_up(conduction[...], conduction_index[i]) - looked_up(
            valence[...], valence_index[i]
        )
        gaps = jnp.where(pair == i, gap, gaps)
    root_weights = jnp.sqrt(4.0 / gaps)
    for k in range(PANELS):
        outbox[k] = elements[:, k * WIDTH : (k + 1) * WIDTH] * root_weights

    a, b = wrap(x - lax.rem(z, 4), 4), wrap(y - z // 4, 4)
    lags, sends = [], []
    for t in range(4):
        na, nb = ((a, b), (b, -a), (-a, -b), (-b, a))[t]
        node = wrap(na, 4) * 4 + wrap(nb, 4)
        lag = jnp.int32(0)
        for (da, db), depth in DEPTHS.items():
            lag = jnp.where(node == da * 4 + db, depth, lag)
        lags.append(lag)
        row = []
        for d in range(4):
            hit = jnp.int32(0)
            for da, db in EDGES[(d - t) % 4]:
                hit = jnp.where(node == da * 4 + db, 1, hit)
            row.append(hit)
        sends.append(row)
    is_root = (a == 0) & (b == 0)
    beside = [(wrap(y + db, 4) * 4 + wrap(x + da, 4)) * 2 + core for da, db in MOVES]

    pl.semaphore_wait(barrier, PANELS + 1)

    @pl.loop(1, PANELS)
    def _(k):
        to = wrap(c + k, PANELS)
        pltpu.make_async_remote_copy(
            src_ref=outbox.at[to],
            dst_ref=inbox.at[c],
            send_sem=box_send,
            recv_sem=box_recv.at[c // 8],
            device_id={"gcol": to},
            device_id_type=MESH,
        ).start()

    pltpu.make_async_copy(outbox.at[c], inbox.at[c], box_recv.at[c // 8]).start()

    def pass_on(side, slot, step):
        pltpu.make_async_remote_copy(
            src_ref=cols.at[slot],
            dst_ref=cols.at[slot],
            send_sem=ring_send.at[side],
            recv_sem=ring_recv.at[side, step],
            device_id={"grow": (ahead, behind)[side]},
            device_id_type=MESH,
        ).start()

    for j in range(SUBS):
        landed(inbox.at[pl.ds(8 * j, 8)], box_recv.at[j])
        for k in range(8):
            cols[z * SUBS + j, k * PAIRS : (k + 1) * PAIRS, :] = inbox[8 * j + k]
        pass_on(0, z * SUBS + j, j)
        pass_on(1, z * SUBS + j, (j + 2) % 4)

    chi_copy.wait()

    @pl.loop(-SUBS, 32 + LAG)
    def _(i):
        q = wrap(i, 4)
        step = (i + 64) // 4 - 15

        def to_tree(slot):
            pltpu.make_async_copy(cols.at[slot], rows.at[core, slot], tree_recv.at[slot]).start()

        @pl.when(is_root & (i < 0))
        def _():
            to_tree(z * SUBS + q)

        @pl.when((i >= 0) & (i < STEPS))
        def _():
            for side, sub, plane in (
                (0, q, wrap(z - step, PLANES)),
                (1, wrap(q + 2, 4), wrap(z + step, PLANES)),
            ):
                slot = plane * SUBS + sub
                landed(cols.at[slot], ring_recv.at[side, i])

                @pl.when(i + SUBS < STEPS)
                def _():
                    pass_on(side, slot, i + SUBS)

                @pl.when(is_root)
                def _():
                    to_tree(slot)

        for t in range(4):
            at = i - lags[t]
            kind = wrap(at - t, 4)
            far = (at + 64) // 4 - 15
            plane = wrap(z + jnp.where(kind == 0, -far, far), PLANES)
            slot = plane * SUBS + t

            @pl.when(
                (at >= -SUBS) & (at < STEPS) & ((kind == 0) | ((kind == 2) & (at >= 0)))
            )
            def _():
                piece = rows.at[core, slot]
                landed(piece, tree_recv.at[slot])
                for d in range(4):

                    @pl.when(sends[t][d] == 1)
                    def _():
                        pltpu.make_async_remote_copy(
                            src_ref=piece,
                            dst_ref=piece,
                            send_sem=tree_send.at[t, d],
                            recv_sem=tree_recv.at[slot],
                            device_id={"gcol": beside[d]},
                            device_id_type=MESH,
                        ).start()

                pltpu.make_async_remote_copy(
                    src_ref=piece,
                    dst_ref=piece,
                    send_sem=twin_send,
                    recv_sem=twin_recv.at[slot],
                    device_id={"gcol": twin},
                    device_id_type=MESH,
                ).start()

        unit = i - LAG

        @pl.when(unit >= 0)
        def _():
            group = unit // 4
            quarter = lax.rem(unit, 4)
            planes = (
                wrap(z - jnp.where(group == 7, 0, group + 1), PLANES),
                wrap(z + group + 1, PLANES),
            )

            @pl.when(quarter == 0)
            def _():
                for h, plane in enumerate(planes):
                    for t in range(SUBS):
                        landed(rows.at[0, plane * SUBS + t], twin_recv.at[plane * SUBS + t])
                    block = cols[pl.ds(plane * SUBS, SUBS)].reshape(SUBS * DEEP, WIDTH)
                    high, low = split(block)
                    cut[0, h * 128 : (h + 1) * 128, :] = high
                    cut[1, h * 128 : (h + 1) * 128, :] = low

            half = quarter // 2
            first = pl.multiple_of(lax.rem(quarter, 2) * 256, 256)
            left = jnp.concatenate(
                [
                    rows[half, pl.ds(plane * SUBS, SUBS), :, pl.ds(first, 256)].reshape(
                        SUBS * DEEP, 256
                    )
                    for plane in planes
                ],
                axis=0,
            )
            high, low = split(left)
            place = pl.ds(pl.multiple_of(quarter * 256, 256), 256)
            out[place, :] += (
                over_pairs(high, cut[0]) + over_pairs(high, cut[1]) + over_pairs(low, cut[0])
            )

    landed(outbox.at[pl.ds(0, PANELS - 1)], box_send)
    for side in range(2):
        landed(cols.at[pl.ds(0, STEPS)], ring_send.at[side])
    for t in range(4):
        for d in range(4):

            @pl.when(sends[t][d] == 1)
            def _():
                landed(rows.at[0, pl.ds(0, PLANES)], tree_send.at[t, d])

    landed(rows.at[0], twin_send)


def per_device(
    pair_elements, valence_index, conduction_index, valence_energy, conduction_energy, chi_in
):
    slots = PLANES * SUBS
    vmem = pl.BlockSpec(memory_space=pltpu.VMEM)
    smem = pl.BlockSpec(memory_space=pltpu.SMEM)
    return pl.pallas_call(
        kernel,
        out_shape=jax.ShapeDtypeStruct(chi_in.shape, jnp.float32),
        in_specs=[smem, smem, vmem, vmem, vmem, pl.BlockSpec(memory_space=pl.ANY)],
        out_specs=vmem,
        scratch_shapes=[
            pltpu.VMEM((PANELS, PAIRS, WIDTH), jnp.float32),
            pltpu.VMEM((PANELS, PAIRS, WIDTH), jnp.float32),
            pltpu.VMEM((slots, DEEP, WIDTH), jnp.float32),
            pltpu.VMEM((2, slots, DEEP, WIDTH), jnp.float32),
            pltpu.VMEM((2, 256, WIDTH), jnp.bfloat16),
            pltpu.SemaphoreType.DMA,
            pltpu.SemaphoreType.DMA((4,)),
            pltpu.SemaphoreType.DMA((2,)),
            pltpu.SemaphoreType.DMA((2, STEPS)),
            pltpu.SemaphoreType.DMA((4, 4)),
            pltpu.SemaphoreType.DMA((slots,)),
            pltpu.SemaphoreType.DMA,
            pltpu.SemaphoreType.DMA((slots,)),
            pltpu.SemaphoreType.DMA,
        ],
        compiler_params=pltpu.CompilerParams(
            collective_id=0, has_side_effects=True, vmem_limit_bytes=40 * 1024 * 1024
        ),
    )(
        valence_index,
        conduction_index,
        valence_energy.reshape(-1, 128),
        conduction_energy.reshape(-1, 128),
        pair_elements,
        chi_in,
    )


def solution(mesh):
    placed = (
        P(("grow", "gcol"), None),
        P(("grow", "gcol")),
        P(("grow", "gcol")),
        P(),
        P(),
        P("grow", "gcol"),
    )
    return jax.shard_map(
        per_device, mesh=mesh, in_specs=placed, out_specs=P("grow", "gcol"), check_vma=False
    )
```

time: 206 us -> 147 us (0.71)
  the two profiles are of different devices: /device:TPU:1 before, /device:TPU:12 now
where the time goes in v1:
time: 147 us
  Pallas kernels  140 us (95%)
  local copies, waits for them, and re-layouts  6.79 us (5%)
    pallas_call x1, Pallas kernels, per_device(): pl.pallas_call(kernel, out_shape=jax.ShapeDtypeStruct(chi_in.shape, jnp.f...  140 us
    unnamed x13, local copies, waits for them, and re-layouts  6.79 us

profile of v1, /device:TPU:12, one launch (start us, length us, event | category | flops | bytes accessed | tf_op | source)
XLA Modules:
  0.0 147.2 jit_solution(4010738649721867204)
XLA Ops:
  0.0 0.0 copy-start
  0.0 1.6 %copy-done = f32[1024,512]{1,0:T(8,128)S(1)} copy-done((f32[1024,512]{1,0:T(8,128)S(1)}, f32[1024,512]{1,0:T(8,128)}, u32[]{:S(2)}) %copy-start) | copy-done | bytes 2097176
  1.6 0.0 copy-start.1
  1.6 0.9 copy-done.1
  2.5 0.0 copy-start.2
  2.5 0.9 copy-done.2
  3.4 0.0 copy-start.3
  3.4 0.7 copy-done.3
  4.2 0.0 copy-start.4
  4.2 0.7 copy-done.4
  4.8 0.0 copy-start.5
  4.8 0.7 copy-done.5
  5.5 140.4 %shard_map.64 = f32[1024,512]{1,0:T(8,128)S(1)} custom-call(s32[4]{0:T(128)S(1)} %copy-done.4, s32[4]{0:T(128)S(1)} %copy-done.5, f32[32,128]{1,0:T(8,128)S(1)} %bitcast.3, f32[256,128]{1,0:T(8,128)S(1)} %bitcast.2, f32[4,16384]{1,0:T(4,128)S(1)} %copy-done.1, f32[1024,512]{1,0:T(8,128)S(1)} %copy-done), custom_call_target="tpu_custom_call" | custom-call | tf_op jit(solution)/shard_map/pallas_call | solution.py:277
  145.8 1.3 copy.8
Async XLA Ops:
  0.0 1.6 %copy-start = (f32[1024,512]{1,0:T(8,128)S(1)}, f32[1024,512]{1,0:T(8,128)}, u32[]{:S(2)}) copy-start(f32[1024,512]{1,0:T(8,128)} %chi.1) | copy-start | bytes 6291460
  1.6 0.9 copy-start.1
  2.5 0.9 copy-start.2
  3.4 0.7 copy-start.3
  4.2 0.7 copy-start.4
  4.8 0.7 copy-start.5

commit v2 on v1

--- a/solution.py
+++ b/solution.py
@@ -13,28 +13,31 @@
 SUBS = 4
 DEEP = PANELS * PAIRS // SUBS
 STEPS = 4 * (PLANES // 2) - 2
-EDGES = (
-    ((0, 0), (1, 0), (1, 2), (1, 3), (2, 0), (2, 1), (2, 2), (2, 3)),
-    ((1, 0), (2, 0)),
-    ((1, 1), (1, 2), (1, 3)),
-    ((1, 0), (1, 3)),
-)
-MOVES = ((1, 0), (0, 1), (-1, 0), (0, -1))
-DEEPEST = 5
-
-
-def depths():
-    found = {(0, 0): 0}
-    for _ in range(16):
-        for (da, db), nodes in zip(MOVES, EDGES):
-            for a, b in nodes:
-                if (a, b) in found:
-                    found[((a + da) % 4, (b + db) % 4)] = found[(a, b)] + 1
-    return found
-
-
-DEPTHS = depths()
-LAG = DEEPEST + 5
+CHILDREN = {
+    (0, 0): ((1, 0),),
+    (1, 0): ((2, 0), (1, 1), (1, 3), (3, 2)),
+    (2, 0): ((2, 1), (3, 0)),
+    (1, 1): ((0, 1),),
+    (1, 3): ((0, 3), (1, 2), (2, 3)),
+    (3, 2): ((0, 2), (2, 2), (3, 1), (3, 3)),
+}
+PORTS = 4
+FAR = (8,)
+NEAR = 8 - (len(FAR) + 1) // 2
+TREE_STEPS = 4 * NEAR
+WAITS = (0, 4, 8, 12)
+SPREAD_AT, TWIN_AT, LAY_AT = 4, 16, 24
+
+ORDER = (0, 1, 2, 3, 7, 4, 5, 6)
+START = 4 * 0 + 3 + WAITS[-1] + 2
+DOUBLE = 4 * ORDER[-1] + 3 + WAITS[-1] + 2 - 4
+LAST = (31 + START + DOUBLE) // 2
+
+
+DEPTHS = {(0, 0): 0}
+for _parent, _children in CHILDREN.items():
+    for _child in _children:
+        DEPTHS[_child] = DEPTHS[_parent] + 1
 
 
 def wrap(value, size):
@@ -64,9 +67,11 @@
 
 
 def kernel(
-    valence_index, conduction_index, valence, conduction, elements, chi, out,
-    outbox, inbox, cols, rows, cut,
-    box_send, box_recv, ring_send, ring_recv, tree_send, tree_recv, twin_send, twin_recv, chi_sem,
+    valence_index_in, conduction_index_in, valence_in, conduction_in, elements_in, chi, out,
+    valence_index, conduction_index, valence, conduction, elements,
+    outbox, inbox, cols, rows, cut, far_box, spread,
+    box_send, box_recv, ring_send, ring_recv, tree_send, tree_recv, twin_send, twin_recv,
+    far_send, far_recv, spread_send, spread_recv, whole_send, whole_recv, in_sem,
 ):
     z = lax.axis_index("grow")
     c = lax.axis_index("gcol")
@@ -74,6 +79,22 @@
     twin = c + 1 - 2 * core
     ahead, behind = wrap(z + 1, PLANES), wrap(z - 1, PLANES)
 
+    loads = [
+        pltpu.make_async_copy(source, target, in_sem.at[i])
+        for i, (source, target) in enumerate(
+            (
+                (valence_index_in, valence_index),
+                (conduction_index_in, conduction_index),
+                (valence_in, valence),
+                (conduction_in, conduction),
+                (elements_in, elements),
+                (chi, out),
+            )
+        )
+    ]
+    for load in loads:
+        load.start()
+
     barrier = pltpu.get_barrier_semaphore()
 
     @pl.loop(1, PANELS)
@@ -82,12 +103,11 @@
             barrier, inc=1, device_id={"gcol": wrap(c + k, PANELS)}, device_id_type=MESH
         )
 
-    for side in (ahead, behind):
+    for side in (ahead, behind, *(wrap(z + far, PLANES) for far in FAR)):
         pl.semaphore_signal(barrier, inc=1, device_id={"grow": side}, device_id_type=MESH)
 
-    chi_copy = pltpu.make_async_copy(chi, out, chi_sem)
-    chi_copy.start()
-
+    for load in loads[:5]:
+        load.wait()
     pair = lax.broadcasted_iota(jnp.int32, (PAIRS, 1), 0)
     gaps = jnp.ones((PAIRS, 1), jnp.float32)
     for i in range(PAIRS):
@@ -106,19 +126,35 @@
         node = wrap(na, 4) * 4 + wrap(nb, 4)
         lag = jnp.int32(0)
         for (da, db), depth in DEPTHS.items():
-            lag = jnp.where(node == da * 4 + db, depth, lag)
+            lag = jnp.where(node == da * 4 + db, WAITS[depth], lag)
         lags.append(lag)
         row = []
-        for d in range(4):
-            hit = jnp.int32(0)
-            for da, db in EDGES[(d - t) % 4]:
-                hit = jnp.where(node == da * 4 + db, 1, hit)
-            row.append(hit)
+        for port in range(PORTS):
+            hit, ca, cb = jnp.int32(0), jnp.int32(0), jnp.int32(0)
+            for (da, db), children in CHILDREN.items():
+                if port < len(children):
+                    here = node == da * 4 + db
+                    hit = jnp.where(here, 1, hit)
+                    ca = jnp.where(here, children[port][0], ca)
+                    cb = jnp.where(here, children[port][1], cb)
+            ca, cb = ((ca, cb), (-cb, ca), (-ca, -cb), (cb, -ca))[t]
+            to = (wrap(z // 4 + cb, 4) * 4 + wrap(lax.rem(z, 4) + ca, 4)) * 2 + core
+            row.append((hit, to))
         sends.append(row)
     is_root = (a == 0) & (b == 0)
-    beside = [(wrap(y + db, 4) * 4 + wrap(x + da, 4)) * 2 + core for da, db in MOVES]
-
-    pl.semaphore_wait(barrier, PANELS + 1)
+
+    pl.semaphore_wait(barrier, PANELS + 1 + len(FAR))
+
+    for k, far in enumerate(FAR):
+        to = wrap(z + far, PLANES)
+        pltpu.make_async_remote_copy(
+            src_ref=outbox.at[pl.ds(2 * to, 2)],
+            dst_ref=far_box.at[k],
+            send_sem=far_send,
+            recv_sem=far_recv,
+            device_id={"grow": to},
+            device_id_type=MESH,
+        ).start()
 
     @pl.loop(1, PANELS)
     def _(k):
@@ -151,9 +187,9 @@
         pass_on(0, z * SUBS + j, j)
         pass_on(1, z * SUBS + j, (j + 2) % 4)
 
-    chi_copy.wait()
-
-    @pl.loop(-SUBS, 32 + LAG)
+    loads[5].wait()
+
+    @pl.loop(-SUBS, LAST + 1)
     def _(i):
         q = wrap(i, 4)
         step = (i + 64) // 4 - 15
@@ -178,7 +214,7 @@
                 def _():
                     pass_on(side, slot, i + SUBS)
 
-                @pl.when(is_root)
+                @pl.when(is_root & (i < TREE_STEPS))
                 def _():
                     to_tree(slot)
 
@@ -190,21 +226,21 @@
             slot = plane * SUBS + t
 
             @pl.when(
-                (at >= -SUBS) & (at < STEPS) & ((kind == 0) | ((kind == 2) & (at >= 0)))
+                (at >= -SUBS) & (at < TREE_STEPS) & ((kind == 0) | ((kind == 2) & (at >= 0)))
             )
             def _():
                 piece = rows.at[core, slot]
                 landed(piece, tree_recv.at[slot])
-                for d in range(4):
-
-                    @pl.when(sends[t][d] == 1)
+                for d, (hit, to) in enumerate(sends[t]):
+
+                    @pl.when(hit == 1)
                     def _():
                         pltpu.make_async_remote_copy(
                             src_ref=piece,
                             dst_ref=piece,
                             send_sem=tree_send.at[t, d],
                             recv_sem=tree_recv.at[slot],
-                            device_id={"gcol": beside[d]},
+                            device_id={"gcol": to},
                             device_id_type=MESH,
                         ).start()
 
@@ -217,86 +253,153 @@
                     device_id_type=MESH,
                 ).start()
 
-        unit = i - LAG
-
-        @pl.when(unit >= 0)
+        line = c // 2
+
+        @pl.when(i == SPREAD_AT)
         def _():
-            group = unit // 4
-            quarter = lax.rem(unit, 4)
+            landed(far_box, far_recv)
+            pltpu.make_async_copy(far_box, spread.at[core, line], spread_recv).start()
+
+            @pl.loop(1, PANELS // 2)
+            def _(k):
+                pltpu.make_async_remote_copy(
+                    src_ref=far_box,
+                    dst_ref=spread.at[core, line],
+                    send_sem=spread_send,
+                    recv_sem=spread_recv,
+                    device_id={"gcol": wrap(c + 2 * k, PANELS)},
+                    device_id_type=MESH,
+                ).start()
+
+        @pl.when(i == TWIN_AT)
+        def _():
+            landed(spread.at[core], spread_recv)
+            pltpu.make_async_remote_copy(
+                src_ref=spread.at[core],
+                dst_ref=spread.at[core],
+                send_sem=whole_send,
+                recv_sem=whole_recv,
+                device_id={"gcol": twin},
+                device_id_type=MESH,
+            ).start()
+
+        @pl.when(i == LAY_AT)
+        def _():
+            landed(spread.at[core], whole_recv)
+
+        for k, far in enumerate(FAR):
+
+            @pl.when(i == LAY_AT + k // 2)
+            def _():
+                plane = wrap(z - far, PLANES)
+
+                @pl.loop(0, SUBS)
+                def _(j):
+                    for m in range(8):
+                        for half in range(2):
+                            rows[half, plane * SUBS + j, m * PAIRS : (m + 1) * PAIRS, :] = spread[
+                                m % 2, j * 4 + m // 2, k, half
+                            ]
+
+        @pl.loop(0, jnp.where(i < DOUBLE, 1, 2))
+        def _(turn):
+            unit = i - START + jnp.maximum(i - DOUBLE, 0) + turn
+            quarter = lax.rem(unit + 64, 4)
+            turn_of = jnp.maximum(unit, 0) // 4
+            group = jnp.int32(0)
+            for turn_at, one in enumerate(ORDER):
+                group = jnp.where(turn_of == turn_at, one, group)
             planes = (
                 wrap(z - jnp.where(group == 7, 0, group + 1), PLANES),
                 wrap(z + group + 1, PLANES),
             )
 
-            @pl.when(quarter == 0)
+            @pl.when((unit >= 0) & (unit < 32) & (quarter == 0))
             def _():
                 for h, plane in enumerate(planes):
-                    for t in range(SUBS):
-                        landed(rows.at[0, plane * SUBS + t], twin_recv.at[plane * SUBS + t])
+                    by_tree = (group < NEAR) if h else (group < NEAR) | (group == 7)
+
+                    @pl.when(by_tree)
+                    def _():
+                        for t in range(SUBS):
+                            slot = plane * SUBS + t
+                            landed(rows.at[0, slot], twin_recv.at[slot])
+
                     block = cols[pl.ds(plane * SUBS, SUBS)].reshape(SUBS * DEEP, WIDTH)
                     high, low = split(block)
                     cut[0, h * 128 : (h + 1) * 128, :] = high
                     cut[1, h * 128 : (h + 1) * 128, :] = low
 
-            half = quarter // 2
-            first = pl.multiple_of(lax.rem(quarter, 2) * 256, 256)
-            left = jnp.concatenate(
-                [
-                    rows[half, pl.ds(plane * SUBS, SUBS), :, pl.ds(first, 256)].reshape(
-                        SUBS * DEEP, 256
-                    )
-                    for plane in planes
-                ],
-                axis=0,
-            )
-            high, low = split(left)
-            place = pl.ds(pl.multiple_of(quarter * 256, 256), 256)
-            out[place, :] += (
-                over_pairs(high, cut[0]) + over_pairs(high, cut[1]) + over_pairs(low, cut[0])
-            )
+            @pl.when((unit >= 0) & (unit < 32))
+            def _():
+                half = quarter // 2
+                first = pl.multiple_of(lax.rem(quarter, 2) * 256, 256)
+                left = jnp.concatenate(
+                    [
+                        rows[half, pl.ds(plane * SUBS, SUBS), :, pl.ds(first, 256)].reshape(
+                            SUBS * DEEP, 256
+                        )
+                        for plane in planes
+                    ],
+                    axis=0,
+                )
+                high, low = split(left)
+                place = pl.ds(pl.multiple_of(quarter * 256, 256), 256)
+                out[place, :] += (
+                    over_pairs(high, cut[0]) + over_pairs(high, cut[1]) + over_pairs(low, cut[0])
+                )
 
     landed(outbox.at[pl.ds(0, PANELS - 1)], box_send)
     for side in range(2):
         landed(cols.at[pl.ds(0, STEPS)], ring_send.at[side])
     for t in range(4):
-        for d in range(4):
-
-            @pl.when(sends[t][d] == 1)
+        for d, (hit, _) in enumerate(sends[t]):
+
+            @pl.when(hit == 1)
             def _():
-                landed(rows.at[0, pl.ds(0, PLANES)], tree_send.at[t, d])
-
-    landed(rows.at[0], twin_send)
+                landed(rows.at[0, pl.ds(0, PLANES - len(FAR))], tree_send.at[t, d])
+
+    landed(rows.at[0, pl.ds(0, (PLANES - len(FAR)) * SUBS)], twin_send)
+    landed(far_box, far_send)
+    landed(spread.at[0, pl.ds(0, PANELS // 2 - 1)], spread_send)
+    landed(spread.at[core], whole_send)
 
 
 def per_device(
     pair_elements, valence_index, conduction_index, valence_energy, conduction_energy, chi_in
 ):
     slots = PLANES * SUBS
-    vmem = pl.BlockSpec(memory_space=pltpu.VMEM)
-    smem = pl.BlockSpec(memory_space=pltpu.SMEM)
     return pl.pallas_call(
         kernel,
         out_shape=jax.ShapeDtypeStruct(chi_in.shape, jnp.float32),
-        in_specs=[smem, smem, vmem, vmem, vmem, pl.BlockSpec(memory_space=pl.ANY)],
-        out_specs=vmem,
+        in_specs=[pl.BlockSpec(memory_space=pltpu.HBM)] * 6,
+        out_specs=pl.BlockSpec(memory_space=pltpu.VMEM),
         scratch_shapes=[
+            pltpu.SMEM((PAIRS,), jnp.int32),
+            pltpu.SMEM((PAIRS,), jnp.int32),
+            pltpu.VMEM((valence_energy.size // 128, 128), jnp.float32),
+            pltpu.VMEM((conduction_energy.size // 128, 128), jnp.float32),
+            pltpu.VMEM(pair_elements.shape, jnp.float32),
             pltpu.VMEM((PANELS, PAIRS, WIDTH), jnp.float32),
             pltpu.VMEM((PANELS, PAIRS, WIDTH), jnp.float32),
             pltpu.VMEM((slots, DEEP, WIDTH), jnp.float32),
             pltpu.VMEM((2, slots, DEEP, WIDTH), jnp.float32),
             pltpu.VMEM((2, 256, WIDTH), jnp.bfloat16),
+            pltpu.VMEM((len(FAR), 2, PAIRS, WIDTH), jnp.float32),
+            pltpu.VMEM((2, PANELS // 2, len(FAR), 2, PAIRS, WIDTH), jnp.float32),
             pltpu.SemaphoreType.DMA,
             pltpu.SemaphoreType.DMA((4,)),
             pltpu.SemaphoreType.DMA((2,)),
             pltpu.SemaphoreType.DMA((2, STEPS)),
-            pltpu.SemaphoreType.DMA((4, 4)),
+            pltpu.SemaphoreType.DMA((4, PORTS)),
             pltpu.SemaphoreType.DMA((slots,)),
             pltpu.SemaphoreType.DMA,
             pltpu.SemaphoreType.DMA((slots,)),
-            pltpu.SemaphoreType.DMA,
+            *[pltpu.SemaphoreType.DMA] * 6,
+            pltpu.SemaphoreType.DMA((6,)),
         ],
         compiler_params=pltpu.CompilerParams(
-            collective_id=0, has_side_effects=True, vmem_limit_bytes=40 * 1024 * 1024
+            collective_id=0, has_side_effects=True, vmem_limit_bytes=63 * 1024 * 1024
         ),
     )(
         valence_index,

time: 147 us -> 95.3 us (0.65)
  the two profiles are of different devices: /device:TPU:12 before, /device:TPU:10 now
where the time goes in v2:
time: 95.3 us; the launch traced here: 95.1 us
  Pallas kernels  92 us (97%)
  local copies, waits for them, and re-layouts  3.08 us (3%)
    pallas_call x1, Pallas kernels, per_device(): pl.pallas_call(kernel, out_shape=jax.ShapeDtypeStruct(chi_in.shape, jnp.f...  92 us
    unnamed x1, local copies, waits for them, and re-layouts  3.08 us

profile of v2, /device:TPU:10, one launch (start us, length us, event | category | flops | bytes accessed | tf_op | source)
XLA Modules:
  0.0 95.1 jit_solution(11873293407832911042)
XLA Ops:
  0.0 92.0 %shard_map.64 = f32[1024,512]{1,0:T(8,128)} custom-call(s32[4]{0:T(128)} %valence_index_in.1, s32[4]{0:T(128)} %conduction_index_in.1, f32[32,128]{1,0:T(8,128)} %bitcast.3, f32[256,128]{1,0:T(8,128)} %bitcast.2, f32[4,16384]{1,0:T(4,128)} %elements_in.1, f32[1024,512]{1,0:T(8,128)} %chi.1), custom_call_target="tpu_custom_call" | custom-call | tf_op jit(solution)/shard_map/pallas_call | solution.py:372
  92.0 3.1 %copy.8 = f32[1024,512]{1,0:T(8,128)} copy(f32[1024,512]{1,0:T(8,128)} %shard_map.64) | data formatting | bytes 4194304

commit v3 on v2

v3 whole, which is shorter than its diff:
```python
import jax
import jax.numpy as jnp
from jax import lax
from jax.experimental import pallas as pl
from jax.experimental.pallas import tpu as pltpu
from jax.sharding import PartitionSpec as P

MESH = pl.DeviceIdType.MESH
PLANES = 16
PANELS = 32
PAIRS = 4
WIDTH = 512
SUBS = 4
DEEP = PANELS * PAIRS // SUBS
STEPS = 4 * (PLANES // 2) - 2
BLOCKS = 4
SLOT = {**{d: 2 * d - 2 for d in range(1, 8)}, **{16 - d: 2 * d - 1 for d in range(1, 8)}, 8: 14, 0: 15}
FIRST_AT, SECOND_AT, TWIN_AT = (0, 1, 3, 5), (3, 7, 11, 15), (9, 14, 18, 22)
START, DOUBLE = 12, 20
LAST = (31 + START + DOUBLE) // 2


def wrap(value, size):
    return lax.rem(value + 4 * size, size)


def looked_up(table, index):
    place = lax.broadcasted_iota(jnp.int32, table.shape, 0) * 128 + lax.broadcasted_iota(
        jnp.int32, table.shape, 1
    )
    return jnp.sum(jnp.where(place == index, table, 0.0), axis=(0, 1), keepdims=True)


def split(value):
    high = value.astype(jnp.bfloat16)
    return high, (value - high.astype(jnp.float32)).astype(jnp.bfloat16)


def over_pairs(left, right):
    return lax.dot_general(
        left, right, (((0,), (0,)), ((), ())), preferred_element_type=jnp.float32
    )


def landed(ref, sem):
    pltpu.make_async_copy(ref, ref, sem).wait()


def kernel(
    valence_index_in, conduction_index_in, valence_in, conduction_in, elements_in, chi, out,
    valence_index, conduction_index, valence, conduction, elements,
    outbox, inbox, row_box, cols, rows, cut,
    box_send, box_recv, ring_send, ring_recv, row_send, row_recv,
    first_send, first_recv, second_send, second_recv, twin_send, twin_recv, in_sem,
):
    z = lax.axis_index("grow")
    c = lax.axis_index("gcol")
    core, x, y = lax.rem(c, 2), lax.rem(c // 2, 4), c // 8
    twin = c + 1 - 2 * core
    ahead, behind = wrap(z + 1, PLANES), wrap(z - 1, PLANES)

    loads = [
        pltpu.make_async_copy(source, target, in_sem.at[i])
        for i, (source, target) in enumerate(
            (
                (valence_index_in, valence_index),
                (conduction_index_in, conduction_index),
                (valence_in, valence),
                (conduction_in, conduction),
                (elements_in, elements),
                (chi, out),
            )
        )
    ]
    for load in loads:
        load.start()

    barrier = pltpu.get_barrier_semaphore()

    @pl.loop(1, PANELS)
    def _(k):
        pl.semaphore_signal(
            barrier, inc=1, device_id={"gcol": wrap(c + k, PANELS)}, device_id_type=MESH
        )

    @pl.loop(1, PLANES)
    def _(k):
        for half in range(2):
            pl.semaphore_signal(
                barrier,
                inc=1,
                device_id={"grow": wrap(z + k, PLANES), "gcol": c - core + half},
                device_id_type=MESH,
            )

    for load in loads[:5]:
        load.wait()
    pair = lax.broadcasted_iota(jnp.int32, (PAIRS, 1), 0)
    gaps = jnp.ones((PAIRS, 1), jnp.float32)
    for i in range(PAIRS):
        gap = looked_up(conduction[...], conduction_index[i]) - looked_up(
            valence[...], valence_index[i]
        )
        gaps = jnp.where(pair == i, gap, gaps)
    root_weights = jnp.sqrt(4.0 / gaps)
    for k in range(PANELS):
        outbox[k] = elements[:, k * WIDTH : (k + 1) * WIDTH] * root_weights

    first, second = jnp.where(core == 0, x, y), jnp.where(core == 0, y, x)

    def at(second_place, first_place):
        line = jnp.where(
            core == 0, second_place * 4 + first_place, first_place * 4 + second_place
        )
        return line * 2 + core

    pl.semaphore_wait(barrier, PANELS - 1 + 2 * (PLANES - 1))

    by_row, by_column = (y * 4 + x) * 2 + core, (x * 4 + y) * 2 + core

    @pl.loop(1, PANELS)
    def _(k):
        to = wrap(c + k, PANELS)
        place = jnp.where(lax.rem(to, 2) == 0, by_row, by_column)
        pltpu.make_async_remote_copy(
            src_ref=outbox.at[to],
            dst_ref=inbox.at[place],
            send_sem=box_send,
            recv_sem=box_recv.at[place // 8],
            device_id={"gcol": to},
            device_id_type=MESH,
        ).start()

    own = jnp.where(core == 0, by_row, by_column)
    pltpu.make_async_copy(outbox.at[c], inbox.at[own], box_recv.at[own // 8]).start()

    for distance, slot in sorted(SLOT.items(), key=lambda item: item[1]):
        to = wrap(z - distance, PLANES)
        for half in range(2):
            source, target = outbox.at[2 * to + half], row_box.at[slot, core]
            arrived = row_recv.at[slot // 4]

            def send(source=source, target=target, arrived=arrived, to=to, half=half):
                pltpu.make_async_remote_copy(
                    src_ref=source,
                    dst_ref=target,
                    send_sem=row_send,
                    recv_sem=arrived,
                    device_id={"grow": to, "gcol": c - core + half},
                    device_id_type=MESH,
                ).start()

            if distance:
                send()
            else:
                pl.when(core != half)(send)

                @pl.when(core == half)
                def _(source=source, target=target, arrived=arrived):
                    pltpu.make_async_copy(source, target, arrived).start()

    def pass_on(side, slot, step):
        pltpu.make_async_remote_copy(
            src_ref=cols.at[slot],
            dst_ref=cols.at[slot],
            send_sem=ring_send.at[side],
            recv_sem=ring_recv.at[side, step],
            device_id={"grow": (ahead, behind)[side]},
            device_id_type=MESH,
        ).start()

    for j in range(SUBS):
        landed(inbox.at[pl.ds(8 * j, 8)], box_recv.at[j])
        for k in range(8):
            cols[z * SUBS + j, k * PAIRS : (k + 1) * PAIRS, :] = inbox[8 * j + k]
        pass_on(0, z * SUBS + j, j)
        pass_on(1, z * SUBS + j, (j + 2) % 4)

    loads[5].wait()

    @pl.loop(-SUBS, LAST + 1)
    def _(i):
        q = wrap(i, 4)
        step = (i + 64) // 4 - 15

        @pl.when((i >= 0) & (i < STEPS))
        def _():
            for side, sub, plane in (
                (0, q, wrap(z - step, PLANES)),
                (1, wrap(q + 2, 4), wrap(z + step, PLANES)),
            ):
                slot = plane * SUBS + sub
                landed(cols.at[slot], ring_recv.at[side, i])

                @pl.when(i + SUBS < STEPS)
                def _():
                    pass_on(side, slot, i + SUBS)

        for block in range(BLOCKS):

            @pl.when(i == FIRST_AT[block])
            def _():
                landed(row_box.at[pl.ds(4 * block, 4)], row_recv.at[block])
                for slot in range(4):
                    for part in range(2):
                        rows[
                            core, block, second, first, slot, part * PAIRS : (part + 1) * PAIRS, :
                        ] = row_box[4 * block + slot, part]
                piece = rows.at[core, block, second, first]
                for k in range(1, 4):
                    pltpu.make_async_remote_copy(
                        src_ref=piece,
                        dst_ref=piece,
                        send_sem=first_send,
                        recv_sem=first_recv.at[block],
                        device_id={"gcol": at(second, wrap(first + k, 4))},
                        device_id_type=MESH,
                    ).start()

            @pl.when(i == SECOND_AT[block])
            def _():
                landed(rows.at[core, block, second, pl.ds(0, 3)], first_recv.at[block])
                piece = rows.at[core, block, second]
                for k in range(1, 4):
                    pltpu.make_async_remote_copy(
                        src_ref=piece,
                        dst_ref=piece,
                        send_sem=second_send,
                        recv_sem=second_recv.at[block],
                        device_id={"gcol": at(wrap(second + k, 4), first)},
                        device_id_type=MESH,
                    ).start()

            @pl.when(i == TWIN_AT[block])
            def _():
                landed(rows.at[core, block, pl.ds(0, 3)], second_recv.at[block])
                for k in range(4):
                    pltpu.make_async_remote_copy(
                        src_ref=rows.at[core, block, k],
                        dst_ref=rows.at[core, block, pl.ds(0, 4), k],
                        send_sem=twin_send,
                        recv_sem=twin_recv.at[block],
                        device_id={"gcol": twin},
                        device_id_type=MESH,
                    ).start()

        @pl.loop(0, jnp.where(i < DOUBLE, 1, 2))
        def _(turn):
            unit = i - START + jnp.maximum(i - DOUBLE, 0) + turn
            quarter = lax.rem(unit + 64, 4)
            group = jnp.maximum(unit, 0) // 4
            block = group // 2
            planes = (
                wrap(z + group + 1, PLANES),
                wrap(z - jnp.where(group == 7, 0, group + 1), PLANES),
            )

            @pl.when((unit >= 0) & (unit < 32) & (lax.rem(unit + 64, 8) == 0))
            def _():
                landed(rows.at[0, block], twin_recv.at[block])

            @pl.when((unit >= 0) & (unit < 32) & (quarter == 0))
            def _():
                for h, plane in enumerate(planes):
                    values = cols[pl.ds(plane * SUBS, SUBS)].reshape(SUBS * DEEP, WIDTH)
                    high, low = split(values)
                    cut[0, h * 128 : (h + 1) * 128, :] = high
                    cut[1, h * 128 : (h + 1) * 128, :] = low

            @pl.when((unit >= 0) & (unit < 32))
            def _():
                half = quarter // 2
                start = pl.multiple_of(lax.rem(quarter, 2) * 256, 256)
                slot = lax.rem(group, 2) * 2
                left = jnp.concatenate(
                    [
                        rows[half, block, :, :, slot + h, :, pl.ds(start, 256)].reshape(
                            SUBS * DEEP, 256
                        )
                        for h in range(2)
                    ],
                    axis=0,
                )
                high, low = split(left)
                place = pl.ds(pl.multiple_of(quarter * 256, 256), 256)
                out[place, :] += (
                    over_pairs(high, cut[0]) + over_pairs(high, cut[1]) + over_pairs(low, cut[0])
                )

    landed(outbox.at[pl.ds(0, PANELS - 1)], box_send)
    for side in range(2):
        landed(cols.at[pl.ds(0, STEPS)], ring_send.at[side])
    landed(inbox.at[pl.ds(0, 2 * PLANES - 1)], row_send)

    landed(rows.at[0, 0, pl.ds(0, 3)], first_send)
    landed(rows.at[0, pl.ds(0, 3)], second_send)
    landed(rows.at[0], twin_send)


def per_device(
    pair_elements, valence_index, conduction_index, valence_energy, conduction_energy, chi_in
):
    return pl.pallas_call(
        kernel,
        out_shape=jax.ShapeDtypeStruct(chi_in.shape, jnp.float32),
        in_specs=[pl.BlockSpec(memory_space=pltpu.HBM)] * 6,
        out_specs=pl.BlockSpec(memory_space=pltpu.VMEM),
        scratch_shapes=[
            pltpu.SMEM((PAIRS,), jnp.int32),
            pltpu.SMEM((PAIRS,), jnp.int32),
            pltpu.VMEM((valence_energy.size // 128, 128), jnp.float32),
            pltpu.VMEM((conduction_energy.size // 128, 128), jnp.float32),
            pltpu.VMEM(pair_elements.shape, jnp.float32),
            pltpu.VMEM((PANELS, PAIRS, WIDTH), jnp.float32),
            pltpu.VMEM((PANELS, PAIRS, WIDTH), jnp.float32),
            pltpu.VMEM((PLANES, 2, PAIRS, WIDTH), jnp.float32),
            pltpu.VMEM((PLANES * SUBS, DEEP, WIDTH), jnp.float32),
            pltpu.VMEM((2, BLOCKS, 4, 4, 4, 2 * PAIRS, WIDTH), jnp.float32),
            pltpu.VMEM((2, 256, WIDTH), jnp.bfloat16),
            pltpu.SemaphoreType.DMA,
            pltpu.SemaphoreType.DMA((4,)),
            pltpu.SemaphoreType.DMA((2,)),
            pltpu.SemaphoreType.DMA((2, STEPS)),
            *[pltpu.SemaphoreType.DMA, pltpu.SemaphoreType.DMA((BLOCKS,))] * 4,
            pltpu.SemaphoreType.DMA((6,)),
        ],
        compiler_params=pltpu.CompilerParams(
            collective_id=0, has_side_effects=True, vmem_limit_bytes=63 * 1024 * 1024
        ),
    )(
        valence_index,
        conduction_index,
        valence_energy.reshape(-1, 128),
        conduction_energy.reshape(-1, 128),
        pair_elements,
        chi_in,
    )


def solution(mesh):
    placed = (
        P(("grow", "gcol"), None),
        P(("grow", "gcol")),
        P(("grow", "gcol")),
        P(),
        P(),
        P("grow", "gcol"),
    )
    return jax.shard_map(
        per_device, mesh=mesh, in_specs=placed, out_specs=P("grow", "gcol"), check_vma=False
    )
```

time: 95.3 us -> 84.7 us (0.89)
  the two profiles are of different devices: /device:TPU:10 before, /device:TPU:1 now
where the time goes in v3:
time: 84.7 us; the launch traced here: 84.5 us
  Pallas kernels  81.4 us (96%)
  local copies, waits for them, and re-layouts  3.08 us (4%)
    pallas_call x1, Pallas kernels, per_device(): pl.pallas_call(kernel, out_shape=jax.ShapeDtypeStruct(chi_in.shape, jnp.f...  81.4 us
    unnamed x1, local copies, waits for them, and re-layouts  3.08 us

profile of v3, /device:TPU:1, one launch (start us, length us, event | category | flops | bytes accessed | tf_op | source)
XLA Modules:
  0.0 84.5 jit_solution(16736616005312483429)
XLA Ops:
  0.0 81.4 %shard_map.64 = f32[1024,512]{1,0:T(8,128)} custom-call(s32[4]{0:T(128)} %valence_index_in.1, s32[4]{0:T(128)} %conduction_index_in.1, f32[32,128]{1,0:T(8,128)} %bitcast.3, f32[256,128]{1,0:T(8,128)} %bitcast.2, f32[4,16384]{1,0:T(4,128)} %elements_in.1, f32[1024,512]{1,0:T(8,128)} %chi.1), custom_call_target="tpu_custom_call" | custom-call | tf_op jit(solution)/shard_map/pallas_call | solution.py:303
  81.5 3.1 %copy.8 = f32[1024,512]{1,0:T(8,128)} copy(f32[1024,512]{1,0:T(8,128)} %shard_map.64) | data formatting | bytes 4194304

commit v4 on v3

--- a/solution.py
+++ b/solution.py
@@ -15,8 +15,9 @@
 STEPS = 4 * (PLANES // 2) - 2
 BLOCKS = 4
 SLOT = {**{d: 2 * d - 2 for d in range(1, 8)}, **{16 - d: 2 * d - 1 for d in range(1, 8)}, 8: 14, 0: 15}
-FIRST_AT, SECOND_AT, TWIN_AT = (0, 1, 3, 5), (3, 7, 11, 15), (9, 14, 18, 22)
-START, DOUBLE = 12, 20
+SWAP_AT = (0, 2, 4, 6)
+FIRST_AT, SECOND_AT, TWIN_AT = (1, 3, 5, 7), (5, 9, 13, 17), (12, 17, 21, 25)
+START, DOUBLE = 15, 16
 LAST = (31 + START + DOUBLE) // 2
 
 
@@ -49,8 +50,9 @@
 def kernel(
     valence_index_in, conduction_index_in, valence_in, conduction_in, elements_in, chi, out,
     valence_index, conduction_index, valence, conduction, elements,
-    outbox, inbox, row_box, cols, rows, cut,
+    outbox, inbox, row_box, swap_box, cols, rows, cut,
     box_send, box_recv, ring_send, ring_recv, row_send, row_recv,
+    swap_send, swap_recv,
     first_send, first_recv, second_send, second_recv, twin_send, twin_recv, in_sem,
 ):
     z = lax.axis_index("grow")
@@ -85,13 +87,9 @@
 
     @pl.loop(1, PLANES)
     def _(k):
-        for half in range(2):
-            pl.semaphore_signal(
-                barrier,
-                inc=1,
-                device_id={"grow": wrap(z + k, PLANES), "gcol": c - core + half},
-                device_id_type=MESH,
-            )
+        pl.semaphore_signal(
+            barrier, inc=1, device_id={"grow": wrap(z + k, PLANES)}, device_id_type=MESH
+        )
 
     for load in loads[:5]:
         load.wait()
@@ -114,7 +112,7 @@
         )
         return line * 2 + core
 
-    pl.semaphore_wait(barrier, PANELS - 1 + 2 * (PLANES - 1))
+    pl.semaphore_wait(barrier, PANELS - 1 + PLANES - 1)
 
     by_row, by_column = (y * 4 + x) * 2 + core, (x * 4 + y) * 2 + core
 
@@ -136,28 +134,18 @@
 
     for distance, slot in sorted(SLOT.items(), key=lambda item: item[1]):
         to = wrap(z - distance, PLANES)
-        for half in range(2):
-            source, target = outbox.at[2 * to + half], row_box.at[slot, core]
-            arrived = row_recv.at[slot // 4]
-
-            def send(source=source, target=target, arrived=arrived, to=to, half=half):
-                pltpu.make_async_remote_copy(
-                    src_ref=source,
-                    dst_ref=target,
-                    send_sem=row_send,
-                    recv_sem=arrived,
-                    device_id={"grow": to, "gcol": c - core + half},
-                    device_id_type=MESH,
-                ).start()
-
-            if distance:
-                send()
-            else:
-                pl.when(core != half)(send)
-
-                @pl.when(core == half)
-                def _(source=source, target=target, arrived=arrived):
-                    pltpu.make_async_copy(source, target, arrived).start()
+        source = outbox.at[pl.ds(2 * to, 2)]
+        if distance:
+            pltpu.make_async_remote_copy(
+                src_ref=source,
+                dst_ref=row_box.at[slot],
+                send_sem=row_send,
+                recv_sem=row_recv.at[slot // 4],
+                device_id={"grow": to},
+                device_id_type=MESH,
+            ).start()
+        else:
+            pltpu.make_async_copy(source, row_box.at[slot], row_recv.at[slot // 4]).start()
 
     def pass_on(side, slot, step):
         pltpu.make_async_remote_copy(
@@ -198,14 +186,30 @@
 
         for block in range(BLOCKS):
 
+            @pl.when(i == SWAP_AT[block])
+            def _():
+                landed(row_box.at[pl.ds(4 * block, 4)], row_recv.at[block])
+                pltpu.make_async_remote_copy(
+                    src_ref=row_box.at[pl.ds(4 * block, 4), 1 - core],
+                    dst_ref=swap_box.at[pl.ds(4 * block, 4)],
+                    send_sem=swap_send,
+                    recv_sem=swap_recv.at[block],
+                    device_id={"gcol": twin},
+                    device_id_type=MESH,
+                ).start()
+
             @pl.when(i == FIRST_AT[block])
             def _():
-                landed(row_box.at[pl.ds(4 * block, 4)], row_recv.at[block])
+                landed(swap_box.at[pl.ds(4 * block, 4)], swap_recv.at[block])
                 for slot in range(4):
-                    for part in range(2):
-                        rows[
-                            core, block, second, first, slot, part * PAIRS : (part + 1) * PAIRS, :
-                        ] = row_box[4 * block + slot, part]
+                    own = row_box[4 * block + slot, core]
+                    other = swap_box[4 * block + slot]
+                    rows[core, block, second, first, slot, :PAIRS, :] = jnp.where(
+                        core == 0, own, other
+                    )
+                    rows[core, block, second, first, slot, PAIRS:, :] = jnp.where(
+                        core == 0, other, own
+                    )
                 piece = rows.at[core, block, second, first]
                 for k in range(1, 4):
                     pltpu.make_async_remote_copy(
@@ -290,7 +294,8 @@
     landed(outbox.at[pl.ds(0, PANELS - 1)], box_send)
     for side in range(2):
         landed(cols.at[pl.ds(0, STEPS)], ring_send.at[side])
-    landed(inbox.at[pl.ds(0, 2 * PLANES - 1)], row_send)
+    landed(row_box.at[pl.ds(0, PLANES - 1)], row_send)
+    landed(swap_box, swap_send)
 
     landed(rows.at[0, 0, pl.ds(0, 3)], first_send)
     landed(rows.at[0, pl.ds(0, 3)], second_send)
@@ -314,6 +319,7 @@
             pltpu.VMEM((PANELS, PAIRS, WIDTH), jnp.float32),
             pltpu.VMEM((PANELS, PAIRS, WIDTH), jnp.float32),
             pltpu.VMEM((PLANES, 2, PAIRS, WIDTH), jnp.float32),
+            pltpu.VMEM((PLANES, PAIRS, WIDTH), jnp.float32),
             pltpu.VMEM((PLANES * SUBS, DEEP, WIDTH), jnp.float32),
             pltpu.VMEM((2, BLOCKS, 4, 4, 4, 2 * PAIRS, WIDTH), jnp.float32),
             pltpu.VMEM((2, 256, WIDTH), jnp.bfloat16),
@@ -321,7 +327,7 @@
             pltpu.SemaphoreType.DMA((4,)),
             pltpu.SemaphoreType.DMA((2,)),
             pltpu.SemaphoreType.DMA((2, STEPS)),
-            *[pltpu.SemaphoreType.DMA, pltpu.SemaphoreType.DMA((BLOCKS,))] * 4,
+            *[pltpu.SemaphoreType.DMA, pltpu.SemaphoreType.DMA((BLOCKS,))] * 5,
             pltpu.SemaphoreType.DMA((6,)),
         ],
         compiler_params=pltpu.CompilerParams(

time: 84.7 us -> 81.9 us (0.967)
  Pallas kernels: 81.4 us -> 78.7 us
    pallas_call x1, Pallas kernels: 81.4 us -> 78.7 us  [per_device(): pl.pallas_call(kernel, out_shape=jax.ShapeDtypeStruct(chi_in.shape, jnp.f...]
where the time goes in v4:
time: 81.9 us; the launch traced here: 81.7 us
  Pallas kernels  78.7 us (96%)
  local copies, waits for them, and re-layouts  3.08 us (4%)
    pallas_call x1, Pallas kernels, per_device(): pl.pallas_call(kernel, out_shape=jax.ShapeDtypeStruct(chi_in.shape, jnp.f...  78.7 us
    unnamed x1, local copies, waits for them, and re-layouts  3.08 us

profile of v4, /device:TPU:1, one launch (start us, length us, event | category | flops | bytes accessed | tf_op | source)
XLA Modules:
  0.0 81.7 jit_solution(1220820938337919497)
XLA Ops:
  0.0 78.7 %shard_map.64 = f32[1024,512]{1,0:T(8,128)} custom-call(s32[4]{0:T(128)} %valence_index_in.1, s32[4]{0:T(128)} %conduction_index_in.1, f32[32,128]{1,0:T(8,128)} %bitcast.3, f32[256,128]{1,0:T(8,128)} %bitcast.2, f32[4,16384]{1,0:T(4,128)} %elements_in.1, f32[1024,512]{1,0:T(8,128)} %chi.1), custom_call_target="tpu_custom_call" | custom-call | tf_op jit(solution)/shard_map/pallas_call | solution.py:308
  78.7 3.1 %copy.8 = f32[1024,512]{1,0:T(8,128)} copy(f32[1024,512]{1,0:T(8,128)} %shard_map.64) | data formatting | bytes 4194304

commit v5 on v4

--- a/solution.py
+++ b/solution.py
@@ -17,8 +17,8 @@
 SLOT = {**{d: 2 * d - 2 for d in range(1, 8)}, **{16 - d: 2 * d - 1 for d in range(1, 8)}, 8: 14, 0: 15}
 SWAP_AT = (0, 2, 4, 6)
 FIRST_AT, SECOND_AT, TWIN_AT = (1, 3, 5, 7), (5, 9, 13, 17), (12, 17, 21, 25)
-START, DOUBLE = 15, 16
-LAST = (31 + START + DOUBLE) // 2
+START, LAST_BLOCK = 15, 27
+LAST = 30
 
 
 def wrap(value, size):
@@ -48,12 +48,12 @@
 
 
 def kernel(
-    valence_index_in, conduction_index_in, valence_in, conduction_in, elements_in, chi, out,
+    valence_index_in, conduction_index_in, valence_in, conduction_in, elements_in, chi, result,
     valence_index, conduction_index, valence, conduction, elements,
-    outbox, inbox, row_box, swap_box, cols, rows, cut,
+    out, outbox, inbox, row_box, swap_box, cols, rows, cut,
     box_send, box_recv, ring_send, ring_recv, row_send, row_recv,
     swap_send, swap_recv,
-    first_send, first_recv, second_send, second_recv, twin_send, twin_recv, in_sem,
+    first_send, first_recv, second_send, second_recv, twin_send, twin_recv, in_sem, out_sem,
 ):
     z = lax.axis_index("grow")
     c = lax.axis_index("gcol")
@@ -113,24 +113,6 @@
         return line * 2 + core
 
     pl.semaphore_wait(barrier, PANELS - 1 + PLANES - 1)
-
-    by_row, by_column = (y * 4 + x) * 2 + core, (x * 4 + y) * 2 + core
-
-    @pl.loop(1, PANELS)
-    def _(k):
-        to = wrap(c + k, PANELS)
-        place = jnp.where(lax.rem(to, 2) == 0, by_row, by_column)
-        pltpu.make_async_remote_copy(
-            src_ref=outbox.at[to],
-            dst_ref=inbox.at[place],
-            send_sem=box_send,
-            recv_sem=box_recv.at[place // 8],
-            device_id={"gcol": to},
-            device_id_type=MESH,
-        ).start()
-
-    own = jnp.where(core == 0, by_row, by_column)
-    pltpu.make_async_copy(outbox.at[c], inbox.at[own], box_recv.at[own // 8]).start()
 
     for distance, slot in sorted(SLOT.items(), key=lambda item: item[1]):
         to = wrap(z - distance, PLANES)
@@ -146,6 +128,24 @@
             ).start()
         else:
             pltpu.make_async_copy(source, row_box.at[slot], row_recv.at[slot // 4]).start()
+
+    by_row, by_column = (y * 4 + x) * 2 + core, (x * 4 + y) * 2 + core
+
+    @pl.loop(1, PANELS)
+    def _(k):
+        to = wrap(c + k, PANELS)
+        place = jnp.where(lax.rem(to, 2) == 0, by_row, by_column)
+        pltpu.make_async_remote_copy(
+            src_ref=outbox.at[to],
+            dst_ref=inbox.at[place],
+            send_sem=box_send,
+            recv_sem=box_recv.at[place // 8],
+            device_id={"gcol": to},
+            device_id_type=MESH,
+        ).start()
+
+    own = jnp.where(core == 0, by_row, by_column)
+    pltpu.make_async_copy(outbox.at[c], inbox.at[own], box_recv.at[own // 8]).start()
 
     def pass_on(side, slot, step):
         pltpu.make_async_remote_copy(
@@ -248,48 +248,67 @@
                         device_id_type=MESH,
                     ).start()
 
-        @pl.loop(0, jnp.where(i < DOUBLE, 1, 2))
-        def _(turn):
-            unit = i - START + jnp.maximum(i - DOUBLE, 0) + turn
-            quarter = lax.rem(unit + 64, 4)
-            group = jnp.maximum(unit, 0) // 4
-            block = group // 2
-            planes = (
-                wrap(z + group + 1, PLANES),
-                wrap(z - jnp.where(group == 7, 0, group + 1), PLANES),
+        def prepare(planes):
+            for h, plane in enumerate(planes):
+                values = cols[pl.ds(plane * SUBS, SUBS)].reshape(SUBS * DEEP, WIDTH)
+                high, low = split(values)
+                cut[0, h * 128 : (h + 1) * 128, :] = high
+                cut[1, h * 128 : (h + 1) * 128, :] = low
+
+        def multiply(block, quarter, slots):
+            half = quarter // 2
+            start = pl.multiple_of(lax.rem(quarter, 2) * 256, 256)
+            left = jnp.concatenate(
+                [
+                    rows[half, block, :, :, slot, :, pl.ds(start, 256)].reshape(SUBS * DEEP, 256)
+                    for slot in slots
+                ],
+                axis=0,
             )
-
-            @pl.when((unit >= 0) & (unit < 32) & (lax.rem(unit + 64, 8) == 0))
+            high, low = split(left)
+            deep = len(slots) * 128
+            place = pl.ds(pl.multiple_of(quarter * 256, 256), 256)
+            out[place, :] += (
+                over_pairs(high, cut[0, :deep])
+                + over_pairs(high, cut[1, :deep])
+                + over_pairs(low, cut[0, :deep])
+            )
+            return place
+
+        @pl.when((i >= START) & (i < LAST_BLOCK))
+        def _():
+            block = (i - START) // 4
+            quarter = lax.rem(i - START, 4)
+
+            @pl.when(quarter == 0)
             def _():
                 landed(rows.at[0, block], twin_recv.at[block])
-
-            @pl.when((unit >= 0) & (unit < 32) & (quarter == 0))
-            def _():
-                for h, plane in enumerate(planes):
-                    values = cols[pl.ds(plane * SUBS, SUBS)].reshape(SUBS * DEEP, WIDTH)
-                    high, low = split(values)
-                    cut[0, h * 128 : (h + 1) * 128, :] = high
-                    cut[1, h * 128 : (h + 1) * 128, :] = low
-
-            @pl.when((unit >= 0) & (unit < 32))
-            def _():
-                half = quarter // 2
-                start = pl.multiple_of(lax.rem(quarter, 2) * 256, 256)
-                slot = lax.rem(group, 2) * 2
-                left = jnp.concatenate(
-                    [
-                        rows[half, block, :, :, slot + h, :, pl.ds(start, 256)].reshape(
-                            SUBS * DEEP, 256
-                        )
-                        for h in range(2)
-                    ],
-                    axis=0,
-                )
-                high, low = split(left)
-                place = pl.ds(pl.multiple_of(quarter * 256, 256), 256)
-                out[place, :] += (
-                    over_pairs(high, cut[0]) + over_pairs(high, cut[1]) + over_pairs(low, cut[0])
-                )
+                near = 2 * block + 1
+                prepare([wrap(z + d, PLANES) for d in (near, -near, near + 1, -near - 1)])
+
+            multiply(block, quarter, range(4))
+
+        @pl.when(i == LAST_BLOCK)
+        def _():
+            landed(rows.at[0, BLOCKS - 1], twin_recv.at[BLOCKS - 1])
+
+        @pl.when(i >= LAST_BLOCK)
+        def _():
+            last = (i - LAST_BLOCK) // 2
+
+            @pl.loop(0, 2)
+            def _(turn):
+                quarter = lax.rem(i - LAST_BLOCK, 2) * 2 + turn
+
+                @pl.when(quarter == 0)
+                def _():
+                    prepare([wrap(z + 7 + last, PLANES), wrap(z - jnp.where(last == 1, 0, 7), PLANES)])
+
+                place = multiply(BLOCKS - 1, quarter, (2 * last, 2 * last + 1))
+
+                @pl.when(last == 1)
+                def _():
+                    pltpu.make_async_copy(out.at[place], result.at[place], out_sem).start()
 
     landed(outbox.at[pl.ds(0, PANELS - 1)], box_send)
     for side in range(2):
@@ -300,6 +319,7 @@
     landed(rows.at[0, 0, pl.ds(0, 3)], first_send)
     landed(rows.at[0, pl.ds(0, 3)], second_send)
     landed(rows.at[0], twin_send)
+    pltpu.make_async_copy(out, result, out_sem).wait()
 
 
 def per_device(
@@ -309,26 +329,28 @@
         kernel,
         out_shape=jax.ShapeDtypeStruct(chi_in.shape, jnp.float32),
         in_specs=[pl.BlockSpec(memory_space=pltpu.HBM)] * 6,
-        out_specs=pl.BlockSpec(memory_space=pltpu.VMEM),
+        out_specs=pl.BlockSpec(memory_space=pltpu.HBM),
         scratch_shapes=[
             pltpu.SMEM((PAIRS,), jnp.int32),
             pltpu.SMEM((PAIRS,), jnp.int32),
             pltpu.VMEM((valence_energy.size // 128, 128), jnp.float32),
             pltpu.VMEM((conduction_energy.size // 128, 128), jnp.float32),
             pltpu.VMEM(pair_elements.shape, jnp.float32),
+            pltpu.VMEM(chi_in.shape, jnp.float32),
             pltpu.VMEM((PANELS, PAIRS, WIDTH), jnp.float32),
             pltpu.VMEM((PANELS, PAIRS, WIDTH), jnp.float32),
             pltpu.VMEM((PLANES, 2, PAIRS, WIDTH), jnp.float32),
             pltpu.VMEM((PLANES, PAIRS, WIDTH), jnp.float32),
             pltpu.VMEM((PLANES * SUBS, DEEP, WIDTH), jnp.float32),
             pltpu.VMEM((2, BLOCKS, 4, 4, 4, 2 * PAIRS, WIDTH), jnp.float32),
-            pltpu.VMEM((2, 256, WIDTH), jnp.bfloat16),
+            pltpu.VMEM((2, 512, WIDTH), jnp.bfloat16),
             pltpu.SemaphoreType.DMA,
             pltpu.SemaphoreType.DMA((4,)),
             pltpu.SemaphoreType.DMA((2,)),
             pltpu.SemaphoreType.DMA((2, STEPS)),
             *[pltpu.SemaphoreType.DMA, pltpu.SemaphoreType.DMA((BLOCKS,))] * 5,
             pltpu.SemaphoreType.DMA((6,)),
+            pltpu.SemaphoreType.DMA,
         ],
         compiler_params=pltpu.CompilerParams(
             collective_id=0, has_side_effects=True, vmem_limit_bytes=63 * 1024 * 1024

time: 81.9 us -> 80.8 us (0.987)
  Pallas kernels: 78.7 us -> 77.5 us
    pallas_call x1, Pallas kernels: 78.7 us -> 77.5 us  [per_device(): pl.pallas_call(kernel, out_shape=jax.ShapeDtypeStruct(chi_in.shape, jnp.f...]
where the time goes in v5:
time: 80.8 us; the launch traced here: 80.6 us
  Pallas kernels  77.5 us (96%)
  local copies, waits for them, and re-layouts  3.08 us (4%)
    pallas_call x1, Pallas kernels, per_device(): pl.pallas_call(kernel, out_shape=jax.ShapeDtypeStruct(chi_in.shape, jnp.f...  77.5 us
    unnamed x1, local copies, waits for them, and re-layouts  3.08 us

profile of v5, /device:TPU:1, one launch (start us, length us, event | category | flops | bytes accessed | tf_op | source)
XLA Modules:
  0.0 80.6 jit_solution(11302608397113269714)
XLA Ops:
  0.0 77.5 %shard_map.64 = f32[1024,512]{1,0:T(8,128)} custom-call(s32[4]{0:T(128)} %valence_index_in.1, s32[4]{0:T(128)} %conduction_index_in.1, f32[32,128]{1,0:T(8,128)} %bitcast.3, f32[256,128]{1,0:T(8,128)} %bitcast.2, f32[4,16384]{1,0:T(4,128)} %elements_in.1, f32[1024,512]{1,0:T(8,128)} %chi.1), custom_call_target="tpu_custom_call" | custom-call | tf_op jit(solution)/shard_map/pallas_call | solution.py:328
  77.5 3.1 %copy.8 = f32[1024,512]{1,0:T(8,128)} copy(f32[1024,512]{1,0:T(8,128)} %shard_map.64) | data formatting | bytes 4194304

commit v6 on v5

--- a/solution.py
+++ b/solution.py
@@ -16,7 +16,7 @@
 BLOCKS = 4
 SLOT = {**{d: 2 * d - 2 for d in range(1, 8)}, **{16 - d: 2 * d - 1 for d in range(1, 8)}, 8: 14, 0: 15}
 SWAP_AT = (0, 2, 4, 6)
-FIRST_AT, SECOND_AT, TWIN_AT = (1, 3, 5, 7), (5, 9, 13, 17), (12, 17, 21, 25)
+FIRST_AT, SECOND_AT, TWIN_AT = (1, 3, 5, 7), (6, 10, 14, 18), (12, 17, 21, 25)
 START, LAST_BLOCK = 15, 27
 LAST = 30
 

time: 80.8 us -> 80.8 us (level)
  no operation moved by 1% of the time
where the time goes in v6:
time: 80.8 us; the launch traced here: 80.6 us
  Pallas kernels  77.5 us (96%)
  local copies, waits for them, and re-layouts  3.08 us (4%)
    pallas_call x1, Pallas kernels, per_device(): pl.pallas_call(kernel, out_shape=jax.ShapeDtypeStruct(chi_in.shape, jnp.f...  77.5 us
    unnamed x1, local copies, waits for them, and re-layouts  3.08 us

profile of v6, /device:TPU:1, one launch (start us, length us, event | category | flops | bytes accessed | tf_op | source)
XLA Modules:
  0.0 80.6 jit_solution(18422254886411500165)
XLA Ops:
  0.0 77.5 %shard_map.64 = f32[1024,512]{1,0:T(8,128)} custom-call(s32[4]{0:T(128)} %valence_index_in.1, s32[4]{0:T(128)} %conduction_index_in.1, f32[32,128]{1,0:T(8,128)} %bitcast.3, f32[256,128]{1,0:T(8,128)} %bitcast.2, f32[4,16384]{1,0:T(4,128)} %elements_in.1, f32[1024,512]{1,0:T(8,128)} %chi.1), custom_call_target="tpu_custom_call" | custom-call | tf_op jit(solution)/shard_map/pallas_call | solution.py:328
  77.5 3.1 %copy.8 = f32[1024,512]{1,0:T(8,128)} copy(f32[1024,512]{1,0:T(8,128)} %shard_map.64) | data formatting | bytes 4194304
